TPU v7x, 256 devices: a whole 4x4x8 slice. The times are simulated.
256 devices in a mesh: row: 8 (over z_hi, y), col: 32 (over x, z_lo, core).
Axes of the slice: x: 4, y: 4, z: 8 (z_hi: 2, z_lo: 4; z = z_hi * 4 + z_lo), core: 2. Of those that a mesh axis runs over, the one named last changes fastest.
Arguments:
- features: bfloat16 [524288, 256], P(('row', 'col')), may hold values from -6 to 6
- tile_values: bfloat16 [65536, 128, 128], P(('row', 'col')), as said below
- tile_rows: int32 [65536], P(('row', 'col')), may hold values from 0 to 511, as said below
- tile_cols: int32 [65536], P(('row', 'col')), may hold values from 0 to 127, as said below
- tile_count: int32 [256], P(('row', 'col')), may hold values from 64 to 256, as said below
- weight: bfloat16 [256, 256], replicated, may hold values from -0.375 to 0.375
- bias: float32 [256], replicated, may hold values from -3 to 3
Outputs:
- activated: bfloat16 [524288, 256], P(('row', 'col'))
Inputs may be any that keep to these rules, and one draw needn't show every extreme that they name: tile_count[d] is the number of live slots of cell d, the first ones of its 256; the largest entry equals 256 in every draw, and every entry is 256, 128 or 64. `tile_values`: nonnegative edge weights. With P = 16, in grid cell d = r * 32 + c: an even slot 2 m has tile_rows // P == c, and an odd slot 2 m + 1 has tile_rows // P == m % 32. With P = 16, in grid cell d = r * 32 + c: an even slot has tile_cols // P == r and tile_cols % P within one of its tile_rows % P.
All inputs are finite; a program needn't handle non-finite values.
Results may differ from a plain program's by a relative error of at most 0.0047.
Values may be sent and summed in bfloat16 or wider, within the bound.
A program may use at most 128 MiB of HBM per device.

v0:
```python
import math

import jax
import jax.numpy as jnp
from jax import lax
from jax.sharding import PartitionSpec as P


def local(features, tile_values, tile_rows, tile_cols, tile_count, weight, bias):
    block_size = tile_values.shape[1]
    rows_here = features.shape[0]
    feat_width = features.shape[1]
    blocks_here = rows_here // block_size
    col_count = lax.axis_size("col")
    half_slots = tile_values.shape[0] // 2
    slot_depth = half_slots // col_count
    live_count = tile_count[0]
    gathered = lax.all_gather(features, "row", axis=0, tiled=True)
    sources = gathered.reshape(-1, block_size, feat_width)
    pair_values = tile_values.reshape(half_slots, 2, block_size, block_size)
    pair_rows = (tile_rows % blocks_here).reshape(half_slots, 2)
    pair_cols = tile_cols.reshape(half_slots, 2)
    pair_index = jnp.arange(half_slots, dtype=jnp.int32)
    other_live = 2 * pair_index + 1 < live_count
    group_size = math.gcd(half_slots, 16)
    offsets = jnp.arange(group_size, dtype=jnp.int32)

    def add_group(group_step, running):
        first_slot = group_step * group_size
        values = lax.dynamic_slice_in_dim(pair_values, first_slot, group_size, 0)[:, 0]
        row_ids = lax.dynamic_slice_in_dim(pair_rows, first_slot, group_size, 0)[:, 0]
        col_ids = lax.dynamic_slice_in_dim(pair_cols, first_slot, group_size, 0)[:, 0]
        product = jnp.einsum(
            "gij,gjf->gif", values, sources[col_ids], preferred_element_type=jnp.float32
        )
        target = jnp.where(2 * (first_slot + offsets) < live_count, row_ids, blocks_here)
        return running.at[target].add(product, mode="drop")

    diag_live = (live_count + 1) // 2
    group_total = (diag_live + group_size - 1) // group_size
    start_sum = jnp.zeros((blocks_here, block_size, feat_width), jnp.float32)
    running = lax.fori_loop(0, group_total, add_group, start_sum)
    other_values = pair_values[:, 1]
    other_ids = pair_rows[:, 1]
    other_sources = sources[pair_cols[:, 1]]
    other_product = jnp.einsum(
        "sij,sjf->sif", other_values, other_sources, preferred_element_type=jnp.float32
    )
    other_product = jnp.where(other_live[:, None, None], other_product, 0.0)
    arrived, arrived_ids = (
        lax.all_to_all(
            other_product.reshape(slot_depth, col_count, block_size, feat_width),
            "col",
            split_axis=1,
            concat_axis=1,
            tiled=True,
        ),
        lax.all_to_all(
            other_ids.astype(jnp.float32).reshape(slot_depth, col_count),
            "col",
            split_axis=1,
            concat_axis=1,
            tiled=True,
        ),
    )
    arrived_sums = arrived.reshape(-1, block_size, feat_width)
    running = running.at[arrived_ids.reshape(-1).astype(jnp.int32)].add(arrived_sums)
    aggregated = running.reshape(rows_here, feat_width).astype(jnp.bfloat16)
    projected = jnp.dot(aggregated, weight, preferred_element_type=jnp.float32) + bias
    return jnp.maximum(projected, 0.0).astype(jnp.bfloat16)


def solution(mesh):
    return jax.shard_map(
        local,
        mesh=mesh,
        in_specs=(
            P(("row", "col"), None),
            P(("row", "col"), None, None),
            P(("row", "col")),
            P(("row", "col")),
            P(("row", "col")),
            P(),
            P(),
        ),
        out_specs=P(("row", "col"), None),
        check_vma=False,
    )
```

profile of v0, /device:TPU:1, one launch (start us, length us, event | category | flops | bytes accessed | tf_op | source)
XLA Modules:
  0.0 641.5 jit_solution(17533069434035848895)
XLA Ops:
  6.5 0.7 all-gather.2.cloned.1.call-update
  7.3 0.7 and_select_fusion
  7.9 0.1 reshape.83
  8.1 0.2 fusion.11
  8.3 0.1 convert_element_type.37
  8.4 0.7 copy.54
  9.1 10.0 %all-to-all-start = ((f32[4,32,1]{0,2,1:T(1,128)}), f32[4,32,1]{0,2,1:T(1,128)S(1)}, u32[]{:S(2)}, u32[]{:S(2)}) async-start(f32[4,32,1]{0,2,1:T(1,128)} %copy.54), calls=%async_computation | async-start | bytes 32768 | tf_op jit(solution)/shard_map/all_to_all | solution.py:58
  19.7 0.8 reshape.85
  20.6 0.2 fusion.10
  20.8 166.0 %all-gather.2.cloned.1.call-done = bf16[16384,256]{1,0:T(8,128)(2,1)} async-done(((bf16[2048,256]{1,0:T(8,128)(2,1)}), bf16[16384,256]{1,0:T(8,128)(2,1)}) %all-gather.2.cloned.1.call-update) | async-done | bytes 8388624 | tf_op jit(solution)/shard_map/all_gather | solution.py:18
  186.8 10.0 %gather_fusion.1 = bf16[128,128,256]{2,1,0:T(8,128)(2,1)} fusion(bf16[128,128,256]{2,1,0:T(8,128)(2,1)} %bitcast.44, s32[1024]{0:T(1024)S(1)} %pad_clamp_fusion.1), kind=kCustom, calls=%fused_computation.1 | custom fusion | bytes 16777728 | tf_op jit(solution)/shard_map/gather | solution.py:45
  196.7 13.0 %convolution_select_fusion = f32[128,256,128]{2,1,0:T(8,128)} fusion(bf16[128,128,256]{2,1,0:T(8,128)(2,1)} %gather_fusion.1, pred[128]{0:T(512)(128)(4,1)S(1)} %add_compare_fusion, bf16[128,2,128,128]{3,2,1,0:T(8,128)(2,1)} %bitcast.46), kind=kOutput, calls=%fused_computation.18 | convolution fusion | flops 1077936128 | bytes 29360256 | tf_op jit(solution)/shard_map/sij,sjf->sif/dot_general | solution.py:46
  209.7 11.6 %copy.61 = f32[4,32,128,256]{2,3,0,1:T(8,128)} copy(f32[4,32,128,256]{2,3,1,0:T(8,128)} %bitcast.43) | data formatting | bytes 33554432 | tf_op jit(solution)/shard_map/reshape | solution.py:52
  221.3 5.8 all-to-all-start.1
  227.2 10.3 %copy.52 = bf16[128,2,128,128]{3,2,0,1:T(8,128)(2,1)} copy(bf16[128,2,128,128]{3,2,1,0:T(8,128)(2,1)} %bitcast.47) | data formatting | bytes 16777216
  237.7 0.1 convert_element_type.43
  237.8 0.1 fusion.9
  237.9 0.2 broadcast_in_dim.25
  238.2 22.2 %while.11 = (s32[]{:T(128)}, f32[16,128,256]{2,1,0:T(8,128)S(1)}, s32[]{:T(128)}, s32[]{:T(128)}, s32[128,2]{0,1:T(2,128)S(1)}, /*index=5*/bf16[128,2,128,128]{3...) while((s32[]{:T(128)}, f32[16,128,256]{2,1,0:T(8,128)S(1)}, ...), condition=%wide.region_2.3_spmd.clone, body=%wide.region_0.2_spmd.clone.sunk | while | flops 134743200 | bytes 12063867 | solution.py:42
  238.3 0.7 fusion.23
  238.9 4.0 gather_fusion
  242.9 2.8 fusion.25
  245.7 3.5 scatter_fusion
  249.3 0.7 fusion.23
  250.0 4.0 gather_fusion
  254.0 2.8 fusion.25
  256.8 3.5 scatter_fusion
  260.3 331.0 %all-to-all-done.1 = f32[4,32,128,256]{2,3,0,1:T(8,128)} async-done(((f32[4,32,128,256]{2,3,0,1:T(8,128)}), f32[4,32,128,256]{2,3,0,1:T(8,128)}, u32[]{:S(2)}, u32[]{:S(2)}) %all-to-all-start.1) | async-done | bytes 16777248 | tf_op jit(solution)/shard_map/all_to_all | solution.py:51
  591.4 17.4 %copy.62 = f32[4,32,128,256]{3,2,1,0:T(8,128)} copy(f32[4,32,128,256]{2,3,0,1:T(8,128)} %all-to-all-done.1) | data formatting | bytes 33554432 | tf_op jit(solution)/shard_map/all_to_all | solution.py:51
  608.8 24.3 %scatter_fusion.1 = f32[16,128,256]{2,1,0:T(8,128)S(1)} fusion(f32[16,128,256]{2,1,0:T(8,128)S(1)} %get-tuple-element.53, s32[128]{0:T(128)S(1)} %fusion.9, f32[128,128,256]{2,1,0:T(8,128)} %bitcast.42), kind=kCustom, calls=%fused_computation.3 | custom fusion | flops 4194304 | bytes 50332160 | tf_op jit(solution)/shard_map/scatter-add | solution.py:67
  633.1 0.1 convert_element_type.40
  633.3 1.4 fusion.8
  (18 shorter events, 0.4 us)
Async XLA Ops:
  6.5 626.7 %copy-start = (bf16[256,256]{1,0:T(8,128)(2,1)S(1)}, bf16[256,256]{1,0:T(8,128)(2,1)}, u32[]{:S(2)}) copy-start(bf16[256,256]{1,0:T(8,128)(2,1)} %param.14) | copy-start | bytes 393220
  6.5 180.3 %all-gather.2.cloned.1.call-start = ((), (), s32[]{:S(2)}) async-start(), calls=%async_computation.2 | async-start | bytes 9437184 | tf_op jit(solution)/shard_map/all_gather | solution.py:18
  9.1 212.2 %all-to-all-start = ((f32[4,32,1]{0,2,1:T(1,128)}), f32[4,32,1]{0,2,1:T(1,128)S(1)}, u32[]{:S(2)}, u32[]{:S(2)}) async-start(f32[4,32,1]{0,2,1:T(1,128)} %copy.54), calls=%async_computation | async-start | bytes 32768 | tf_op jit(solution)/shard_map/all_to_all | solution.py:58
  221.3 370.1 %all-to-all-start.1 = ((f32[4,32,128,256]{2,3,0,1:T(8,128)}), f32[4,32,128,256]{2,3,0,1:T(8,128)}, u32[]{:S(2)}, u32[]{:S(2)}) async-start(f32[4,32,128,256]{2,3,0,1:T(8,128)} %copy.61), calls=%async_computation.1 | async-start | bytes 33554432 | tf_op jit(solution)/shard_map/all_to_all | solution.py:51
  608.8 24.5 %copy-start.1 = (f32[256]{0:T(256)S(1)}, f32[256]{0:T(256)}, u32[]{:S(2)}) copy-start(f32[256]{0:T(256)} %param.15) | copy-start | bytes 3076
Sparse Core Ops, SparseCore 0:
  10.0 176.7 all-gather.1
where the time goes:
time: 643 us; the launch traced here: 642 us
  waiting for transfers between devices  498 us (77%)
  local copies, waits for them, and re-layouts  59.7 us (9%)
  other arithmetic  34 us (5%)
  matrix products  19.9 us (3%)
  starting transfers between devices  15.9 us (2%)
  between operations  14.2 us (2%)
    all_to_all x1, waiting for transfers between devices, local(): lax.all_to_all(other_product.reshape(slot_depth, col_count, block_size, f...  331 us
    all_gather x1, waiting for transfers between devices, local(): gathered = lax.all_gather(features, 'row', axis=0, tiled=True)  166 us
    scatter-add x1, other arithmetic, local(): running.at[arrived_ids.reshape(-1).astype(jnp.int32)].add(arrived_sums)  24.3 us
    all_to_all x1, local copies, waits for them, and re-layouts, local(): lax.all_to_all(other_product.reshape(slot_depth, col_count, block_size, f...  17.4 us
    dot_general x1, matrix products, local(): jnp.einsum('sij,sjf->sif', other_values, other_sources, preferred_element...  13 us
  transfers between devices with their start and end apart: 3, of which 2 were waited for; matrix products, arithmetic and copies ran while one was open for 11% of the time, Pallas kernels for 0%

commit v1 on v0

v1 whole, which is shorter than its diff:
```python
import jax
import jax.numpy as jnp
from jax import lax
from jax.experimental import pallas as pl
from jax.experimental.pallas import tpu as pltpu
from jax.sharding import PartitionSpec as P

MESH = pl.DeviceIdType.MESH
BLOCK = 128
PER_DEV = 16
PAIRS = 128
HALF = 128
ROWS = PER_DEV * BLOCK
GROUP = 16
N_X, N_Z, N_Y, N_HI = 4, 4, 4, 2
LEVELS = 4
CHUNK = 16


def near_kernel(row_ref, col_ref, live_ref, feat_ref, tiles_ref, acc_ref, held, sem):
    live = live_ref[0]
    copies = [
        pltpu.make_async_copy(
            tiles_ref.at[pl.ds(c * CHUNK, CHUNK), 0], held.at[pl.ds(c * CHUNK, CHUNK)], sem.at[c]
        )
        for c in range(PAIRS // CHUNK)
    ]
    for c, copy in enumerate(copies):
        pl.when(c * CHUNK < live)(copy.start)
    acc_ref[...] = jnp.zeros_like(acc_ref)
    for c, copy in enumerate(copies):

        @pl.when(c * CHUNK < live)
        def _():
            copy.wait()

            def add(s, carry):
                slot = c * CHUNK + s
                out = pl.ds(pl.multiple_of(row_ref[slot] * BLOCK, BLOCK), BLOCK)
                src = pl.ds(pl.multiple_of(col_ref[slot] * BLOCK, BLOCK), BLOCK)
                acc_ref[out, :] += jnp.dot(
                    held[slot], feat_ref[src, :], preferred_element_type=jnp.float32
                )
                return carry

            lax.fori_loop(0, CHUNK, add, 0, unroll=4)


def near(row_ids, col_ids, live, features, tiles):
    vmem = pl.BlockSpec(memory_space=pltpu.VMEM)
    smem = pl.BlockSpec(memory_space=pltpu.SMEM)
    return pl.pallas_call(
        near_kernel,
        out_shape=jax.ShapeDtypeStruct((ROWS, 2 * HALF), jnp.float32),
        in_specs=[smem, smem, smem, vmem, pl.BlockSpec(memory_space=pl.ANY)],
        out_specs=vmem,
        scratch_shapes=[
            pltpu.VMEM((PAIRS, BLOCK, BLOCK), jnp.bfloat16),
            pltpu.SemaphoreType.DMA((PAIRS // CHUNK,)),
        ],
        compiler_params=pltpu.CompilerParams(vmem_limit_bytes=24 * 2**20),
    )(row_ids, col_ids, live, features, tiles)


def far_kernel(
    src_ref,
    feat_ref,
    ids_ref,
    weight_ref,
    bias_ref,
    tiles_ref,
    near_ref,
    out_ref,
    gath0,
    gath1,
    tiles,
    ids,
    pick,
    xs,
    xr,
    zs,
    zr,
    own,
    near_sum,
    proj,
    tile_sem,
    near_sem,
    hi_send,
    hi_recv,
    y_send,
    y_recv,
    id_send,
    id_recv,
    x_send,
    x_recv,
    z_send,
    z_recv,
):
    row = lax.axis_index("row")
    col = lax.axis_index("col")
    z_hi, y = row // N_Y, lax.rem(row, N_Y)
    x, z, k = col // (2 * N_Z), lax.rem(col // 2, N_Z), lax.rem(col, 2)
    mine = x * 2 + k
    gath = (gath0, gath1)

    def plane(o):
        return lax.rem(x + o // 2, N_X) * 2 + lax.rem(k + lax.rem(o, 2), 2)

    def plane_dev(p):
        return {"row": row, "col": (p // 2) * (2 * N_Z) + z * 2 + lax.rem(p, 2)}

    def y_dev(d):
        return {"row": z_hi * N_Y + lax.rem(y + d, N_Y), "col": col}

    hi_row = (1 - z_hi) * N_Y + y
    hi_dev = {"row": hi_row, "col": col}

    def z_dev(d):
        return {"row": row, "col": x * (2 * N_Z) + lax.rem(z + d, N_Z) * 2 + k}

    load_tiles = pltpu.make_async_copy(tiles_ref.at[:, 1], tiles, tile_sem)
    load_tiles.start()
    load_near = pltpu.make_async_copy(near_ref, near_sum, near_sem)
    load_near.start()

    barrier = pltpu.get_barrier_semaphore()
    peers = [hi_dev] + [y_dev(d) for d in range(1, N_Y)] + [z_dev(d) for d in range(1, N_Z)]
    peers += [plane_dev(plane(o)) for o in range(1, 8)]
    for peer in peers:
        pl.semaphore_signal(barrier, inc=1, device_id=peer, device_id_type=MESH)
    pl.semaphore_wait(barrier, len(peers))

    def share(h, r):
        return gath[h].at[pl.ds(r * PER_DEV, PER_DEV)]

    def copy(src, dst, send, recv, peer):
        return pltpu.make_async_remote_copy(
            src_ref=src, dst_ref=dst, send_sem=send, recv_sem=recv, device_id=peer, device_id_type=MESH
        )

    def hi_copy(h):
        half = feat_ref.at[:, :, pl.ds(h * HALF, HALF)]
        return copy(half, share(h, row), hi_send.at[h], hi_recv.at[h], hi_dev)

    def y_copy(h, d, part):
        src = feat_ref.at[:, :, pl.ds(h * HALF, HALF)] if part == 0 else share(h, hi_row)
        dst = share(h, row if part == 0 else hi_row)
        sems = y_send.at[h, part, d - 1], y_recv.at[h, part, d - 1]
        return copy(src, dst, *sems, y_dev(d))

    def y_arrival(h, d, part):
        back = lax.rem(y + N_Y - d, N_Y)
        r = (z_hi if part == 0 else 1 - z_hi) * N_Y + back
        sems = y_send.at[h, part, d - 1], y_recv.at[h, part, d - 1]
        return copy(share(h, r), share(h, r), *sems, y_dev(d))

    def hi_arrival(h):
        dst = share(h, hi_row)
        return copy(dst, dst, hi_send.at[h], hi_recv.at[h], hi_dev)

    def id_copy(o):
        p = plane(o)
        return copy(ids_ref.at[p], ids.at[mine], id_send.at[p], id_recv.at[mine], plane_dev(p))

    def id_arrival(o):
        p = plane(o)
        return copy(ids.at[p], ids.at[p], id_send.at[p], id_recv.at[p], plane_dev(p))

    def x_copy(h, j, o):
        p = plane(o)
        return copy(xs.at[h, j, o - 1], xr.at[h, j, mine], x_send.at[h, j, p], x_recv.at[h, j, mine], plane_dev(p))

    def x_arrival(h, j, o):
        p = plane(o)
        return copy(xr.at[h, j, p], xr.at[h, j, p], x_send.at[h, j, p], x_recv.at[h, j, p], plane_dev(p))

    def z_copy(h, j):
        return copy(zs.at[h, j], zr.at[h, j], z_send.at[h, j], z_recv.at[h, j], z_dev(j + 1))

    def over(n, body):
        def step(o, carry):
            body(o)
            return carry

        lax.fori_loop(1, n, step, 0)

    hi_copy(0).start()
    for d in (1, 3, 2):
        y_copy(0, d, 0).start()
    over(8, lambda o: id_copy(o).start())
    for h in range(2):
        for b in range(PER_DEV):
            gath[h][row * PER_DEV + b] = feat_ref[b, :, pl.ds(h * HALF, HALF)]
        gath[h][8 * PER_DEV] = jnp.zeros((BLOCK, HALF), jnp.bfloat16)
    ids[mine] = ids_ref[mine]

    over(8, lambda o: id_arrival(o).wait_recv())

    def build(j):
        to = lax.rem(z + 1 + j, N_Z)
        line = lax.broadcasted_iota(jnp.int32, (PER_DEV * GROUP, BLOCK), 0)
        lane = lax.broadcasted_iota(jnp.int32, (PER_DEV * GROUP, BLOCK), 1)
        same = lax.rem(line, GROUP) == lax.rem(lane, GROUP)
        for c in range(N_X):
            block = ids[2 * c, pl.ds(to, 1), :] + ids[2 * c + 1, pl.ds(to, 1), :]
            hit = same & (line // GROUP == block)
            pick[j, :, pl.ds(c * BLOCK, BLOCK)] = jnp.where(hit, 1.0, 0.0).astype(jnp.bfloat16)

    for j in range(N_Z):
        build(j)

    hi_arrival(0).wait_recv()
    for d in (1, 3, 2):
        y_copy(0, d, 1).start()
    hi_copy(1).start()
    load_tiles.wait()
    for d in (1, 3, 2):
        y_arrival(0, d, 0).wait_recv()
    for d in (1, 3, 2):
        y_arrival(0, d, 1).wait_recv()
    for d in (1, 3, 2):
        y_copy(1, d, 0).start()

    def product(h, j, p, lv):
        to = lax.rem(z + 1 + j, N_Z)
        slot = lv * 32 + (p // 2) * (2 * N_Z) + to * 2 + lax.rem(p, 2)
        out = jnp.dot(tiles[slot], gath[h][src_ref[slot]], preferred_element_type=jnp.float32)
        return out.astype(jnp.bfloat16)

    def multiply(h, j):
        def one(o):
            for lv in range(LEVELS):
                xs[h, j, o - 1, lv] = product(h, j, plane(o), lv)
            x_copy(h, j, o).start()

        over(8, one)
        for lv in range(LEVELS):
            xr[h, j, mine, lv] = product(h, j, mine, lv)

    def combine(h, j):
        over(8, lambda o: x_arrival(h, j, o).wait_recv())

        def some(g, carry):
            rows = pl.ds(pl.multiple_of(g * GROUP, GROUP), GROUP)
            arrived = xr[h, j, :, :, rows, :].reshape(8 * LEVELS * GROUP, HALF)
            total = jnp.dot(pick[j], arrived, preferred_element_type=jnp.float32)
            total = total.reshape(PER_DEV, GROUP, HALF)
            if j < N_Z - 1:
                zs[h, j, :, rows, :] = total.astype(jnp.bfloat16)
            else:
                own[h, :, rows, :] = total
            return carry

        lax.fori_loop(0, BLOCK // GROUP, some, 0)
        if j < N_Z - 1:
            z_copy(h, j).start()

    def finish(h):
        for j in range(N_Z - 1):
            z_copy(h, j).wait_recv()

        def some(b, carry):
            total = own[h, b] + near_sum[pl.ds(pl.multiple_of(b * BLOCK, BLOCK), BLOCK), pl.ds(h * HALF, HALF)]
            for j in range(N_Z - 1):
                total += zr[h, j, b].astype(jnp.float32)
            part = jnp.dot(
                total.astype(jnp.bfloat16),
                weight_ref[pl.ds(h * HALF, HALF), :],
                preferred_element_type=jnp.float32,
            )
            rows = pl.ds(pl.multiple_of(b * BLOCK, BLOCK), BLOCK)
            if h == 0:
                proj[rows, :] = part
            else:
                out_ref[rows, :] = jnp.maximum(proj[rows, :] + part + bias_ref[...], 0.0).astype(jnp.bfloat16)
            return carry

        lax.fori_loop(0, PER_DEV, some, 0)

    multiply(0, 0)
    multiply(0, 1)
    hi_arrival(1).wait_recv()
    for d in (1, 3, 2):
        y_copy(1, d, 1).start()
    multiply(0, 2)
    multiply(0, 3)
    for j in range(N_Z - 1):
        combine(0, j)
    for part in range(2):
        for d in (1, 3, 2):
            y_arrival(1, d, part).wait_recv()
    for j in range(N_Z):
        multiply(1, j)
    combine(0, 3)
    load_near.wait()
    combine(1, 0)
    combine(1, 1)
    finish(0)
    combine(1, 2)
    combine(1, 3)
    finish(1)

    over(8, lambda o: id_copy(o).wait_send())
    for h in range(2):
        hi_copy(h).wait_send()
        for part in range(2):
            for d in (1, 3, 2):
                y_copy(h, d, part).wait_send()
        for j in range(N_Z):
            over(8, lambda o: x_copy(h, j, o).wait_send())
        for j in range(N_Z - 1):
            z_copy(h, j).wait_send()


def far(src_blocks, features, ids, weight, bias, tiles, near_sum):
    vmem = pl.BlockSpec(memory_space=pltpu.VMEM)
    smem = pl.BlockSpec(memory_space=pltpu.SMEM)
    hbm = pl.BlockSpec(memory_space=pl.ANY)
    dma = pltpu.SemaphoreType.DMA
    return pl.pallas_call(
        far_kernel,
        out_shape=jax.ShapeDtypeStruct((ROWS, 2 * HALF), jnp.bfloat16),
        in_specs=[smem, vmem, vmem, vmem, vmem, hbm, hbm],
        out_specs=vmem,
        scratch_shapes=[
            pltpu.VMEM((8 * PER_DEV + 1, BLOCK, HALF), jnp.bfloat16),
            pltpu.VMEM((8 * PER_DEV + 1, BLOCK, HALF), jnp.bfloat16),
            pltpu.VMEM((PAIRS, BLOCK, BLOCK), jnp.bfloat16),
            pltpu.VMEM((8, 8, BLOCK), jnp.int32),
            pltpu.VMEM((N_Z, PER_DEV * GROUP, 8 * LEVELS * GROUP), jnp.bfloat16),
            pltpu.VMEM((2, N_Z, 7, LEVELS, BLOCK, HALF), jnp.bfloat16),
            pltpu.VMEM((2, N_Z, 8, LEVELS, BLOCK, HALF), jnp.bfloat16),
            pltpu.VMEM((2, N_Z - 1, PER_DEV, BLOCK, HALF), jnp.bfloat16),
            pltpu.VMEM((2, N_Z - 1, PER_DEV, BLOCK, HALF), jnp.bfloat16),
            pltpu.VMEM((2, PER_DEV, BLOCK, HALF), jnp.float32),
            pltpu.VMEM((ROWS, 2 * HALF), jnp.float32),
            pltpu.VMEM((ROWS, 2 * HALF), jnp.float32),
            dma,
            dma,
            dma((2,)),
            dma((2,)),
            dma((2, 2, N_Y - 1)),
            dma((2, 2, N_Y - 1)),
            dma((8,)),
            dma((8,)),
            dma((2, N_Z, 8)),
            dma((2, N_Z, 8)),
            dma((2, N_Z - 1)),
            dma((2, N_Z - 1)),
        ],
        compiler_params=pltpu.CompilerParams(
            collective_id=0, has_side_effects=True, vmem_limit_bytes=56 * 2**20
        ),
    )(src_blocks, features, ids, weight, bias, tiles, near_sum)


def local(features, tile_values, tile_rows, tile_cols, tile_count, weight, bias):
    tiles = tile_values.reshape(PAIRS, 2, BLOCK, BLOCK)
    pair_rows = lax.rem(tile_rows, PER_DEV).reshape(PAIRS, 2)
    pair_cols = tile_cols.reshape(PAIRS, 2)
    near_live = (tile_count + 1) // 2
    near_sum = near(pair_rows[:, 0], lax.rem(pair_cols[:, 0], PER_DEV), near_live, features, tiles)

    pair_index = jnp.arange(PAIRS, dtype=jnp.int32)
    src_blocks = jnp.where(2 * pair_index + 1 < tile_count[0], pair_cols[:, 1], 8 * PER_DEV)
    core = lax.rem(lax.axis_index("col"), 2)
    by_place = pair_rows[:, 1].reshape(LEVELS, N_X, N_Z, 2).transpose(1, 3, 2, 0).reshape(8, N_Z, LEVELS)
    spread = jnp.broadcast_to(by_place[:, :, None, :, None], (8, N_Z, 2, LEVELS, GROUP))
    at_core = (jnp.arange(2, dtype=jnp.int32) == core)[None, None, :, None, None]
    ids = jnp.where(at_core, spread, 0).reshape(8, N_Z, BLOCK)
    ids = jnp.pad(ids, ((0, 0), (0, 8 - N_Z), (0, 0)))
    return far(src_blocks, features.reshape(PER_DEV, BLOCK, -1), ids, weight, bias.reshape(1, -1), tiles, near_sum)


def solution(mesh):
    return jax.shard_map(
        local,
        mesh=mesh,
        in_specs=(
            P(("row", "col"), None),
            P(("row", "col"), None, None),
            P(("row", "col")),
            P(("row", "col")),
            P(("row", "col")),
            P(),
            P(),
        ),
        out_specs=P(("row", "col"), None),
        check_vma=False,
    )
```

time: 643 us -> 205 us (0.32)
  the two profiles are of different devices: /device:TPU:1 before, /device:TPU:103 now
where the time goes in v1:
time: 205 us
  Pallas kernels  192 us (94%)
  local copies, waits for them, and re-layouts  10.9 us (5%)
    pallas_call x1, Pallas kernels, far(): pl.pallas_call(far_kernel, out_shape=jax.ShapeDtypeStruct((ROWS, 2 * HALF...  184 us
    pallas_call x1, Pallas kernels, near(): pl.pallas_call(near_kernel, out_shape=jax.ShapeDtypeStruct((ROWS, 2 * HAL...  8.4 us
    unnamed x7, local copies, waits for them, and re-layouts  8.21 us

profile of v1, /device:TPU:103, one launch (start us, length us, event | category | flops | bytes accessed | tf_op | source)
XLA Modules:
  0.0 204.8 jit_solution(6723247682906922467)
XLA Ops:
  0.7 0.1 broadcast_in_dim.31
  0.8 0.1 broadcast_in_dim.32
  0.9 0.7 compare_select_fusion.2
  1.5 0.1 reshape.29
  1.7 0.2 slice_reduce_fusion.1
  1.9 0.2 reshape_squeeze.3
  2.0 0.2 copy.12
  2.3 0.8 reshape.27
  3.1 0.2 slice_reduce_fusion
  3.3 0.5 compare_select_fusion
  3.8 0.1 broadcast_in_dim.35
  3.9 0.1 broadcast_in_dim.36
  4.0 0.6 pad.4.ids_ref
  4.6 0.0 copy-start
  4.6 3.4 %copy-done = bf16[256,128,128]{2,1,0:T(8,128)(2,1)S(1)} copy-done((bf16[256,128,128]{2,1,0:T(8,128)(2,1)S(1)}, bf16[256,128,128]{2,1,0:T(8,128)(2,1)}, u32[]{:S(2)}) %copy-start) | copy-done | bytes 8388632
  8.0 0.0 copy-start.2
  8.0 1.2 copy-done.2
  9.2 8.4 %shard_map.73.near_ref = f32[2048,256]{1,0:T(8,128)S(1)} custom-call(s32[128]{0:T(128)S(1)} %get-tuple-element.7.row_ref, s32[128]{0:T(128)S(1)} %get-tuple-element.9.col_ref, s32[1]{0:T(128)S(6)} %select_n.16.live_ref, bf16[2048,256]{1,0:T(8,128)(2,1)S(1)} %copy-done.2, bf16[128,2,128,128]{3,2,1,0:T(8,128)(2,1)S(1)} %bitcast.8), custom_call_target="tpu_custom_call" | custom-call | tf_op jit(solution)/shard_map/pallas_call | solution.py:52
  17.6 0.0 copy-start.1
  17.7 1.3 copy-done.1
  19.0 183.6 %shard_map.74 = bf16[2048,256]{1,0:T(8,128)(2,1)} custom-call(s32[128]{0:T(128)} %get-tuple-element.10.src_ref, bf16[16,128,256]{2,1,0:T(8,128)(2,1)} %bitcast.9, s32[8,8,128]{2,1,0:T(8,128)} %pad.4.ids_ref, bf16[256,256]{1,0:T(8,128)(2,1)} %weight_ref.1, f32[1,256]{1,0:T(1,128)} %bitcast.12, bf16[128,2,128,128]{3,2,1,0:T(8,128)(2,1)} %bitcast.7, ...), custom_call_target="tpu_custom_call" | custom-call | tf_op jit(solution)/shard_map/pallas_call | solution.py:320
  202.6 2.3 %copy.16 = bf16[2048,256]{1,0:T(8,128)(2,1)} copy(bf16[2048,256]{1,0:T(8,128)(2,1)} %shard_map.74) | data formatting | bytes 2097152
  (3 shorter events, 0.0 us)
Async XLA Ops:
  4.6 3.4 %copy-start = (bf16[256,128,128]{2,1,0:T(8,128)(2,1)S(1)}, bf16[256,128,128]{2,1,0:T(8,128)(2,1)}, u32[]{:S(2)}) copy-start(bf16[256,128,128]{2,1,0:T(8,128)(2,1)} %param.8) | copy-start | bytes 25165828
  8.0 1.2 copy-start.2
  17.6 1.4 copy-start.1

commit v2 on v1

v2 whole, which is shorter than its diff:
```python
import jax
import jax.numpy as jnp
from jax import lax
from jax.experimental import pallas as pl
from jax.experimental.pallas import tpu as pltpu
from jax.sharding import PartitionSpec as P

MESH = pl.DeviceIdType.MESH
BLOCK = 128
PER_DEV = 16
PAIRS = 128
HALF = 128
ROWS = PER_DEV * BLOCK
GROUP = 16
N_X, N_Z, N_Y, N_HI = 4, 4, 4, 2
LEVELS = 4
PART = 64
STEPS = (2, 1, 3, 0)


def far_kernel(
    count_ref,
    col_ref,
    feat_ref,
    rows_ref,
    weight_ref,
    bias_ref,
    tiles_ref,
    out_ref,
    gath0,
    gath1,
    feat,
    near_tiles,
    far_tiles,
    weight,
    bias,
    ids,
    pick,
    near_pick,
    near_prod,
    near_sum,
    xs,
    xr,
    zs,
    zr,
    own,
    proj,
    load_sem,
    share_sem,
    hi_send,
    hi_recv,
    y_send,
    y_recv,
    id_send,
    id_recv,
    x_send,
    x_recv,
    z_send,
    z_recv,
):
    row = lax.axis_index("row")
    col = lax.axis_index("col")
    z_hi, y = row // N_Y, lax.rem(row, N_Y)
    x, z, k = col // (2 * N_Z), lax.rem(col // 2, N_Z), lax.rem(col, 2)
    mine = x * 2 + k
    gath = (gath0, gath1)
    live = count_ref[0]

    def plane(o):
        return lax.rem(x + o // 2, N_X) * 2 + lax.rem(k + lax.rem(o, 2), 2)

    def plane_dev(p):
        return {"row": row, "col": (p // 2) * (2 * N_Z) + z * 2 + lax.rem(p, 2)}

    def y_dev(d):
        return {"row": z_hi * N_Y + lax.rem(y + d, N_Y), "col": col}

    hi_row = (1 - z_hi) * N_Y + y
    hi_dev = {"row": hi_row, "col": col}

    def z_dev(d):
        return {"row": row, "col": x * (2 * N_Z) + lax.rem(z + d, N_Z) * 2 + k}

    loads = [
        pltpu.make_async_copy(src, dst, load_sem.at[i])
        for i, (src, dst) in enumerate(
            (
                (feat_ref, feat.at[pl.ds(0, PER_DEV)]),
                (rows_ref, ids.at[mine]),
                (tiles_ref.at[:, 0], near_tiles),
                (tiles_ref.at[:, 1], far_tiles),
                (weight_ref, weight),
                (bias_ref, bias),
            )
        )
    ]
    load_feat, load_rows, load_near, load_far, load_weight, load_bias = loads
    for load in loads:
        load.start()

    barrier = pltpu.get_barrier_semaphore()
    peers = [hi_dev] + [y_dev(d) for d in range(1, N_Y)] + [z_dev(d) for d in range(1, N_Z)]
    peers += [plane_dev(plane(o)) for o in range(1, 8)]
    for peer in peers:
        pl.semaphore_signal(barrier, inc=1, device_id=peer, device_id_type=MESH)
    feat[PER_DEV] = jnp.zeros((BLOCK, 2 * HALF), jnp.bfloat16)
    for h in range(2):
        gath[h][8 * PER_DEV] = jnp.zeros((BLOCK, HALF), jnp.bfloat16)
    load_feat.wait()
    load_rows.wait()
    pl.semaphore_wait(barrier, len(peers))

    def share(h, r):
        return gath[h].at[pl.ds(r * PER_DEV, PER_DEV)]

    def half(h):
        return feat.at[pl.ds(0, PER_DEV), :, pl.ds(h * HALF, HALF)]

    def copy(src, dst, send, recv, peer):
        return pltpu.make_async_remote_copy(
            src_ref=src, dst_ref=dst, send_sem=send, recv_sem=recv, device_id=peer, device_id_type=MESH
        )

    def hi_copy(h):
        return copy(half(h), share(h, row), hi_send.at[h], hi_recv.at[h], hi_dev)

    def y_copy(h, d, part):
        src = half(h) if part == 0 else share(h, hi_row)
        dst = share(h, row if part == 0 else hi_row)
        sems = y_send.at[h, part, d - 1], y_recv.at[h, part, d - 1]
        return copy(src, dst, *sems, y_dev(d))

    def y_arrival(h, d, part):
        back = lax.rem(y + N_Y - d, N_Y)
        r = (z_hi if part == 0 else 1 - z_hi) * N_Y + back
        sems = y_send.at[h, part, d - 1], y_recv.at[h, part, d - 1]
        return copy(share(h, r), share(h, r), *sems, y_dev(d))

    def hi_arrival(h):
        dst = share(h, hi_row)
        return copy(dst, dst, hi_send.at[h], hi_recv.at[h], hi_dev)

    def id_copy(o):
        p = plane(o)
        return copy(ids.at[mine], ids.at[mine], id_send.at[p], id_recv.at[mine], plane_dev(p))

    def id_arrival(o):
        p = plane(o)
        return copy(ids.at[p], ids.at[p], id_send.at[p], id_recv.at[p], plane_dev(p))

    def levels(u):
        j = min(u, N_Z - 1)
        return (j, range(LEVELS)) if u < N_Z - 1 else (j, range(2 * (u - j), 2 * (u - j) + 2))

    def x_copy(h, u, o):
        p = plane(o)
        j, lvs = levels(u)
        at = pl.ds(lvs[0], len(lvs))
        return copy(
            xs.at[h, j, o - 1, at], xr.at[h, j, mine, at], x_send.at[h, u, p], x_recv.at[h, u, mine], plane_dev(p)
        )

    def x_arrival(h, u, o):
        p = plane(o)
        j, lvs = levels(u)
        dst = xr.at[h, j, p, pl.ds(lvs[0], len(lvs))]
        return copy(dst, dst, x_send.at[h, u, p], x_recv.at[h, u, p], plane_dev(p))

    def z_copy(h, j):
        return copy(zs.at[h, j], zr.at[h, j], z_send.at[h, j], z_recv.at[h, j], z_dev(STEPS[j]))

    def over(n, body):
        def step(o, carry):
            body(o)
            return carry

        lax.fori_loop(1, n, step, 0)

    hi_copy(0).start()
    for d in (1, 3, 2):
        y_copy(0, d, 0).start()
    over(8, lambda o: id_copy(o).start())
    keeps = [pltpu.make_async_copy(half(h), share(h, row), share_sem.at[h]) for h in range(2)]
    for keep in keeps:
        keep.start()

    line = lax.broadcasted_iota(jnp.int32, (PER_DEV * GROUP, BLOCK), 0)
    lane = lax.broadcasted_iota(jnp.int32, (PER_DEV * GROUP, BLOCK), 1)
    same_row = lax.rem(line, GROUP) == lax.rem(lane, GROUP)
    line_block = (line // GROUP).astype(jnp.float32)

    def spread(p, wanted):
        chosen = jnp.where(wanted, 1.0, 0.0).astype(jnp.bfloat16)
        return jnp.dot(ids[p].astype(jnp.bfloat16), chosen, preferred_element_type=jnp.float32)[0:1, :]

    def picker(block):
        return jnp.where(same_row & (line_block == block), 1.0, 0.0).astype(jnp.bfloat16)

    def near(a):
        for c in range(PART * GROUP // BLOCK):
            slot = a * PART + c * (BLOCK // GROUP) + lane // GROUP
            near_pick[:, pl.ds(c * BLOCK, BLOCK)] = picker(spread(mine, line == 2 * slot))

        def multiply_near(s, carry):
            for i in range(4):
                slot = 2 * (a * PART + 4 * s + i)
                src = jnp.where(slot < live, lax.rem(col_ref[slot], PER_DEV), PER_DEV)
                out = jnp.dot(near_tiles[a * PART + 4 * s + i], feat[src], preferred_element_type=jnp.float32)
                near_prod[4 * s + i] = out.astype(jnp.bfloat16)
            return carry

        lax.fori_loop(0, PART // 4, multiply_near, 0)

        def some(g, carry):
            rows = pl.ds(pl.multiple_of(g * GROUP, GROUP), GROUP)
            parts = near_prod[:, rows, :].reshape(PART * GROUP, 2 * HALF)
            total = jnp.dot(near_pick[...], parts, preferred_element_type=jnp.float32)
            total = total.reshape(PER_DEV, GROUP, 2 * HALF)
            near_sum[:, rows, :] = total if a == 0 else near_sum[:, rows, :] + total
            return carry

        lax.fori_loop(0, BLOCK // GROUP, some, 0)

    load_near.wait()
    near(0)
    hi_arrival(0).wait_recv()
    for d in (1, 3, 2):
        y_copy(0, d, 1).start()
    hi_copy(1).start()
    near(1)

    over(8, lambda o: id_arrival(o).wait_recv())
    for j in range(N_Z):
        to = lax.rem(z + STEPS[j], N_Z)
        slot = lax.rem(lane, BLOCK // 2) // GROUP * 32 + x * (2 * N_Z) + to * 2 + k
        for c in range(N_X):
            block = 0.0
            for i in range(2):
                wanted = (line == 2 * slot + 1) & (lane // (BLOCK // 2) == i)
                block += spread(2 * c + i, wanted)
            pick[j, :, pl.ds(c * BLOCK, BLOCK)] = picker(block)

    load_far.wait()
    for keep in keeps:
        keep.wait()
    for part in range(2):
        for d in (1, 3, 2):
            y_arrival(0, d, part).wait_recv()
    for d in (1, 3, 2):
        y_copy(1, d, 0).start()

    def product(h, j, p, lv):
        to = lax.rem(z + STEPS[j], N_Z)
        slot = lv * 32 + (p // 2) * (2 * N_Z) + to * 2 + lax.rem(p, 2)
        src = jnp.where(2 * slot + 1 < live, col_ref[2 * slot + 1], 8 * PER_DEV)
        out = jnp.dot(far_tiles[slot], gath[h][src], preferred_element_type=jnp.float32)
        return out.astype(jnp.bfloat16)

    def multiply(h, u):
        j, lvs = levels(u)

        def one(o):
            for lv in lvs:
                xs[h, j, o - 1, lv] = product(h, j, plane(o), lv)
            x_copy(h, u, o).start()

        over(8, one)
        for lv in lvs:
            xr[h, j, mine, lv] = product(h, j, mine, lv)

    def combine(h, j):
        for u in (j,) if j < N_Z - 1 else (j, j + 1):
            over(8, lambda o: x_arrival(h, u, o).wait_recv())

        def some(g, carry):
            rows = pl.ds(pl.multiple_of(g * GROUP, GROUP), GROUP)
            arrived = xr[h, j, :, :, rows, :].reshape(8 * LEVELS * GROUP, HALF)
            total = jnp.dot(pick[j], arrived, preferred_element_type=jnp.float32)
            total = total.reshape(PER_DEV, GROUP, HALF)
            if j < N_Z - 1:
                zs[h, j, :, rows, :] = total.astype(jnp.bfloat16)
            else:
                own[h, :, rows, :] = total
            return carry

        lax.fori_loop(0, BLOCK // GROUP, some, 0)
        if j < N_Z - 1:
            z_copy(h, j).start()

    def finish(h):
        for j in range(N_Z - 1):
            z_copy(h, j).wait_recv()

        def some(b, carry):
            total = own[h, b] + near_sum[b, :, pl.ds(h * HALF, HALF)]
            for j in range(N_Z - 1):
                total += zr[h, j, b].astype(jnp.float32)
            part = jnp.dot(
                total.astype(jnp.bfloat16),
                weight[pl.ds(h * HALF, HALF), :],
                preferred_element_type=jnp.float32,
            )
            rows = pl.ds(pl.multiple_of(b * BLOCK, BLOCK), BLOCK)
            if h == 0:
                proj[rows, :] = part
            else:
                out_ref[rows, :] = jnp.maximum(proj[rows, :] + part + bias[...], 0.0).astype(jnp.bfloat16)
            return carry

        lax.fori_loop(0, PER_DEV, some, 0)

    multiply(0, 0)
    multiply(0, 1)
    hi_arrival(1).wait_recv()
    for d in (1, 3, 2):
        y_copy(1, d, 1).start()
    multiply(0, 2)
    multiply(0, 3)
    combine(0, 0)
    combine(0, 1)
    for part in range(2):
        for d in (1, 3, 2):
            y_arrival(1, d, part).wait_recv()
    multiply(1, 0)
    combine(0, 2)
    multiply(1, 1)
    multiply(1, 2)
    multiply(0, 4)
    multiply(1, 3)
    multiply(1, 4)
    load_weight.wait()
    load_bias.wait()
    combine(1, 0)
    combine(1, 1)
    combine(1, 2)
    combine(0, 3)
    finish(0)
    combine(1, 3)
    finish(1)

    over(8, lambda o: id_copy(o).wait_send())
    for h in range(2):
        hi_copy(h).wait_send()
        for part in range(2):
            for d in (1, 3, 2):
                y_copy(h, d, part).wait_send()
        for u in range(N_Z + 1):
            over(8, lambda o: x_copy(h, u, o).wait_send())
        for j in range(N_Z - 1):
            z_copy(h, j).wait_send()


def far(count, cols, features, rows, weight, bias, tiles):
    vmem = pl.BlockSpec(memory_space=pltpu.VMEM)
    smem = pl.BlockSpec(memory_space=pltpu.SMEM)
    hbm = pl.BlockSpec(memory_space=pl.ANY)
    dma = pltpu.SemaphoreType.DMA
    return pl.pallas_call(
        far_kernel,
        out_shape=jax.ShapeDtypeStruct((ROWS, 2 * HALF), jnp.bfloat16),
        in_specs=[smem, smem, hbm, hbm, hbm, hbm, hbm],
        out_specs=vmem,
        scratch_shapes=[
            pltpu.VMEM((8 * PER_DEV + 1, BLOCK, HALF), jnp.bfloat16),
            pltpu.VMEM((8 * PER_DEV + 1, BLOCK, HALF), jnp.bfloat16),
            pltpu.VMEM((PER_DEV + 1, BLOCK, 2 * HALF), jnp.bfloat16),
            pltpu.VMEM((PAIRS, BLOCK, BLOCK), jnp.bfloat16),
            pltpu.VMEM((PAIRS, BLOCK, BLOCK), jnp.bfloat16),
            pltpu.VMEM((2 * HALF, 2 * HALF), jnp.bfloat16),
            pltpu.VMEM((1, 2 * HALF), jnp.float32),
            pltpu.VMEM((8, 8, 2 * PAIRS), jnp.float32),
            pltpu.VMEM((N_Z, PER_DEV * GROUP, 8 * LEVELS * GROUP), jnp.bfloat16),
            pltpu.VMEM((PER_DEV * GROUP, PART * GROUP), jnp.bfloat16),
            pltpu.VMEM((PART, BLOCK, 2 * HALF), jnp.bfloat16),
            pltpu.VMEM((PER_DEV, BLOCK, 2 * HALF), jnp.float32),
            pltpu.VMEM((2, N_Z, 7, LEVELS, BLOCK, HALF), jnp.bfloat16),
            pltpu.VMEM((2, N_Z, 8, LEVELS, BLOCK, HALF), jnp.bfloat16),
            pltpu.VMEM((2, N_Z - 1, PER_DEV, BLOCK, HALF), jnp.bfloat16),
            pltpu.VMEM((2, N_Z - 1, PER_DEV, BLOCK, HALF), jnp.bfloat16),
            pltpu.VMEM((2, PER_DEV, BLOCK, HALF), jnp.float32),
            pltpu.VMEM((ROWS, 2 * HALF), jnp.float32),
            dma((6,)),
            dma((2,)),
            dma((2,)),
            dma((2,)),
            dma((2, 2, N_Y - 1)),
            dma((2, 2, N_Y - 1)),
            dma((8,)),
            dma((8,)),
            dma((2, N_Z + 1, 8)),
            dma((2, N_Z + 1, 8)),
            dma((2, N_Z - 1)),
            dma((2, N_Z - 1)),
        ],
        compiler_params=pltpu.CompilerParams(
            collective_id=0, has_side_effects=True, vmem_limit_bytes=60 * 2**20
        ),
    )(count, cols, features, rows, weight, bias, tiles)


def local(features, tile_values, tile_rows, tile_cols, tile_count, weight, bias):
    tiles = tile_values.reshape(PAIRS, 2, BLOCK, BLOCK)
    rows = jnp.broadcast_to(lax.rem(tile_rows, PER_DEV).astype(jnp.float32), (8, 2 * PAIRS))
    blocks = features.reshape(PER_DEV, BLOCK, 2 * HALF)
    return far(tile_count, tile_cols, blocks, rows, weight, bias.reshape(1, -1), tiles)


def solution(mesh):
    return jax.shard_map(
        local,
        mesh=mesh,
        in_specs=(
            P(("row", "col"), None),
            P(("row", "col"), None, None),
            P(("row", "col")),
            P(("row", "col")),
            P(("row", "col")),
            P(),
            P(),
        ),
        out_specs=P(("row", "col"), None),
        check_vma=False,
    )
```

time: 205 us -> 178 us (0.87)
  the two profiles are of different devices: /device:TPU:103 before, /device:TPU:1 now
where the time goes in v2:
time: 178 us
  Pallas kernels  174 us (98%)
  local copies, waits for them, and re-layouts  2.86 us (2%)
    pallas_call x1, Pallas kernels, far(): pl.pallas_call(far_kernel, out_shape=jax.ShapeDtypeStruct((ROWS, 2 * HALF...  174 us

profile of v2, /device:TPU:1, one launch (start us, length us, event | category | flops | bytes accessed | tf_op | source)
XLA Modules:
  0.0 178.2 jit_solution(11536882776646101203)
XLA Ops:
  0.7 0.7 fusion.1
  1.3 0.6 broadcast_in_dim.3.rows_ref
  1.9 174.0 %shard_map.73 = bf16[2048,256]{1,0:T(8,128)(2,1)} custom-call(s32[1]{0:T(128)S(6)} %copy.9.count_ref, s32[256]{0:T(256)} %col_ref.1, bf16[16,128,256]{2,1,0:T(8,128)(2,1)} %bitcast.4, f32[8,256]{1,0:T(8,128)} %broadcast_in_dim.3.rows_ref, bf16[256,256]{1,0:T(8,128)(2,1)} %weight_ref.1, f32[1,256]{1,0:T(1,128)} %bitcast.5, bf16[128,2,128,128]{3,2,1,0:T(8,128)(2,1)} %bitcast.3), custom_call_target="tpu_custom_call" | custom-call | tf_op jit(solution)/shard_map/pallas_call | solution.py:358
  175.9 2.3 %copy.10 = bf16[2048,256]{1,0:T(8,128)(2,1)} copy(bf16[2048,256]{1,0:T(8,128)(2,1)} %shard_map.73) | data formatting | bytes 2097152

commit v3 on v2

--- a/solution.py
+++ b/solution.py
@@ -14,6 +14,7 @@
 GROUP = 16
 N_X, N_Z, N_Y, N_HI = 4, 4, 4, 2
 LEVELS = 4
+SOME = 8
 PART = 64
 STEPS = (2, 1, 3, 0)
 
@@ -99,7 +100,7 @@
         load.start()
 
     barrier = pltpu.get_barrier_semaphore()
-    peers = [hi_dev] + [y_dev(d) for d in range(1, N_Y)] + [z_dev(d) for d in range(1, N_Z)]
+    peers = [hi_dev, y_dev(1), y_dev(N_Y - 1)] + [z_dev(d) for d in range(1, N_Z)]
     peers += [plane_dev(plane(o)) for o in range(1, 8)]
     for peer in peers:
         pl.semaphore_signal(barrier, inc=1, device_id=peer, device_id_type=MESH)
@@ -121,24 +122,58 @@
             src_ref=src, dst_ref=dst, send_sem=send, recv_sem=recv, device_id=peer, device_id_type=MESH
         )
 
-    def hi_copy(h):
-        return copy(half(h), share(h, row), hi_send.at[h], hi_recv.at[h], hi_dev)
-
-    def y_copy(h, d, part):
-        src = half(h) if part == 0 else share(h, hi_row)
-        dst = share(h, row if part == 0 else hi_row)
-        sems = y_send.at[h, part, d - 1], y_recv.at[h, part, d - 1]
-        return copy(src, dst, *sems, y_dev(d))
-
-    def y_arrival(h, d, part):
-        back = lax.rem(y + N_Y - d, N_Y)
-        r = (z_hi if part == 0 else 1 - z_hi) * N_Y + back
-        sems = y_send.at[h, part, d - 1], y_recv.at[h, part, d - 1]
-        return copy(share(h, r), share(h, r), *sems, y_dev(d))
-
-    def hi_arrival(h):
-        dst = share(h, hi_row)
-        return copy(dst, dst, hi_send.at[h], hi_recv.at[h], hi_dev)
+    def place(h, hi, at_y, first, blocks):
+        return gath[h].at[pl.ds((hi * N_Y + at_y) * PER_DEV + first, blocks)]
+
+    def hi_copy(h, c):
+        src = feat.at[pl.ds(c * SOME, SOME), :, pl.ds(h * HALF, HALF)]
+        return copy(src, place(h, z_hi, y, c * SOME, SOME), hi_send.at[h, c], hi_recv.at[h, c], hi_dev)
+
+    def hi_arrival(h, c):
+        dst = place(h, 1 - z_hi, y, c * SOME, SOME)
+        return copy(dst, dst, hi_send.at[h, c], hi_recv.at[h, c], hi_dev)
+
+    def piece(t):
+        return (z_hi, 0, PER_DEV) if t == 0 else (1 - z_hi, (t - 1) * SOME, SOME)
+
+    def y_copy(h, t, up):
+        hi, first, blocks = piece(t)
+        dst = place(h, hi, y, first, blocks)
+        src = half(h) if t == 0 else dst
+        return copy(src, dst, y_send.at[h, t, 0, up], y_recv.at[h, t, 0, up], y_dev(1 if up else N_Y - 1))
+
+    def y_arrival(h, t, up):
+        hi, first, blocks = piece(t)
+        dst = place(h, hi, lax.rem(y + (N_Y - 1 if up else 1), N_Y), first, blocks)
+        return copy(dst, dst, y_send.at[h, t, 0, up], y_recv.at[h, t, 0, up], y_dev(1))
+
+    def on_copy(h, t, up):
+        hi, first, blocks = piece(t)
+        part = place(h, hi, lax.rem(y + (N_Y - 1 if up else 1), N_Y), first + (1 - up) * (blocks // 2), blocks // 2)
+        return copy(part, part, y_send.at[h, t, 1, up], y_recv.at[h, t, 1, up], y_dev(1 if up else N_Y - 1))
+
+    def on_arrival(h, t, up):
+        hi, first, blocks = piece(t)
+        part = place(h, hi, lax.rem(y + 2, N_Y), first + (1 - up) * (blocks // 2), blocks // 2)
+        return copy(part, part, y_send.at[h, t, 1, up], y_recv.at[h, t, 1, up], y_dev(1))
+
+    def send_on(h, t):
+        for up in (0, 1):
+            y_copy(h, t, up).start()
+
+    def pass_on(h, t):
+        for up in (0, 1):
+            y_arrival(h, t, up).wait_recv()
+            on_copy(h, t, up).start()
+
+    def hi_then_y(h, c):
+        hi_arrival(h, c).wait_recv()
+        send_on(h, c + 1)
+
+    def gathered(h):
+        for t in range(3):
+            for up in (0, 1):
+                on_arrival(h, t, up).wait_recv()
 
     def id_copy(o):
         p = plane(o)
@@ -176,9 +211,9 @@
 
         lax.fori_loop(1, n, step, 0)
 
-    hi_copy(0).start()
-    for d in (1, 3, 2):
-        y_copy(0, d, 0).start()
+    hi_copy(0, 0).start()
+    hi_copy(0, 1).start()
+    send_on(0, 0)
     over(8, lambda o: id_copy(o).start())
     keeps = [pltpu.make_async_copy(half(h), share(h, row), share_sem.at[h]) for h in range(2)]
     for keep in keeps:
@@ -223,12 +258,8 @@
 
     load_near.wait()
     near(0)
-    hi_arrival(0).wait_recv()
-    for d in (1, 3, 2):
-        y_copy(0, d, 1).start()
-    hi_copy(1).start()
-    near(1)
-
+    pass_on(0, 0)
+    hi_then_y(0, 0)
     over(8, lambda o: id_arrival(o).wait_recv())
     for j in range(N_Z):
         to = lax.rem(z + STEPS[j], N_Z)
@@ -243,11 +274,13 @@
     load_far.wait()
     for keep in keeps:
         keep.wait()
-    for part in range(2):
-        for d in (1, 3, 2):
-            y_arrival(0, d, part).wait_recv()
-    for d in (1, 3, 2):
-        y_copy(1, d, 0).start()
+    hi_then_y(0, 1)
+    hi_copy(1, 0).start()
+    hi_copy(1, 1).start()
+    pass_on(0, 1)
+    pass_on(0, 2)
+    send_on(1, 0)
+    gathered(0)
 
     def product(h, j, p, lv):
         to = lax.rem(z + STEPS[j], N_Z)
@@ -311,16 +344,16 @@
 
     multiply(0, 0)
     multiply(0, 1)
-    hi_arrival(1).wait_recv()
-    for d in (1, 3, 2):
-        y_copy(1, d, 1).start()
+    hi_then_y(1, 0)
     multiply(0, 2)
+    pass_on(1, 0)
+    hi_then_y(1, 1)
     multiply(0, 3)
     combine(0, 0)
+    pass_on(1, 1)
+    pass_on(1, 2)
     combine(0, 1)
-    for part in range(2):
-        for d in (1, 3, 2):
-            y_arrival(1, d, part).wait_recv()
+    gathered(1)
     multiply(1, 0)
     combine(0, 2)
     multiply(1, 1)
@@ -328,10 +361,11 @@
     multiply(0, 4)
     multiply(1, 3)
     multiply(1, 4)
+    combine(1, 0)
+    near(1)
+    combine(1, 1)
     load_weight.wait()
     load_bias.wait()
-    combine(1, 0)
-    combine(1, 1)
     combine(1, 2)
     combine(0, 3)
     finish(0)
@@ -340,10 +374,12 @@
 
     over(8, lambda o: id_copy(o).wait_send())
     for h in range(2):
-        hi_copy(h).wait_send()
-        for part in range(2):
-            for d in (1, 3, 2):
-                y_copy(h, d, part).wait_send()
+        for c in range(2):
+            hi_copy(h, c).wait_send()
+        for t in range(3):
+            for up in (0, 1):
+                y_copy(h, t, up).wait_send()
+                on_copy(h, t, up).wait_send()
         for u in range(N_Z + 1):
             over(8, lambda o: x_copy(h, u, o).wait_send())
         for j in range(N_Z - 1):
@@ -381,10 +417,10 @@
             pltpu.VMEM((ROWS, 2 * HALF), jnp.float32),
             dma((6,)),
             dma((2,)),
-            dma((2,)),
-            dma((2,)),
-            dma((2, 2, N_Y - 1)),
-            dma((2, 2, N_Y - 1)),
+            dma((2, 2)),
+            dma((2, 2)),
+            dma((2, 3, 2, 2)),
+            dma((2, 3, 2, 2)),
             dma((8,)),
             dma((8,)),
             dma((2, N_Z + 1, 8)),

time: 178 us -> 167 us (0.938); the launches traced: 178 us -> 164 us
  Pallas kernels: 174 us -> 160 us
    pallas_call x1, Pallas kernels: 174 us -> 160 us  [far(): pl.pallas_call(far_kernel, out_shape=jax.ShapeDtypeStruct((ROWS, 2 * HALF...]
where the time goes in v3:
time: 167 us; the launch traced here: 164 us
  Pallas kernels  160 us (96%)
  local copies, waits for them, and re-layouts  2.86 us (2%)
    pallas_call x1, Pallas kernels, far(): pl.pallas_call(far_kernel, out_shape=jax.ShapeDtypeStruct((ROWS, 2 * HALF...  160 us

profile of v3, /device:TPU:1, one launch (start us, length us, event | category | flops | bytes accessed | tf_op | source)
XLA Modules:
  0.0 164.1 jit_solution(15597868014334930299)
XLA Ops:
  0.7 0.7 fusion.1
  1.3 0.6 broadcast_in_dim.3.rows_ref
  1.9 159.9 %shard_map.73 = bf16[2048,256]{1,0:T(8,128)(2,1)} custom-call(s32[1]{0:T(128)S(6)} %copy.9.count_ref, s32[256]{0:T(256)} %col_ref.1, bf16[16,128,256]{2,1,0:T(8,128)(2,1)} %bitcast.4, f32[8,256]{1,0:T(8,128)} %broadcast_in_dim.3.rows_ref, bf16[256,256]{1,0:T(8,128)(2,1)} %weight_ref.1, f32[1,256]{1,0:T(1,128)} %bitcast.5, bf16[128,2,128,128]{3,2,1,0:T(8,128)(2,1)} %bitcast.3), custom_call_target="tpu_custom_call" | custom-call | tf_op jit(solution)/shard_map/pallas_call | solution.py:394
  161.8 2.3 %copy.10 = bf16[2048,256]{1,0:T(8,128)(2,1)} copy(bf16[2048,256]{1,0:T(8,128)(2,1)} %shard_map.73) | data formatting | bytes 2097152

commit v4 on v3

--- a/solution.py
+++ b/solution.py
@@ -14,9 +14,10 @@
 GROUP = 16
 N_X, N_Z, N_Y, N_HI = 4, 4, 4, 2
 LEVELS = 4
-SOME = 8
+DUOS = 8
+SOME = 4
+PARTS = 4
 PART = 64
-STEPS = (2, 1, 3, 0)
 
 
 def far_kernel(
@@ -30,7 +31,10 @@
     out_ref,
     gath0,
     gath1,
+    gath2,
+    gath3,
     feat,
+    packs,
     near_tiles,
     far_tiles,
     weight,
@@ -64,8 +68,13 @@
     z_hi, y = row // N_Y, lax.rem(row, N_Y)
     x, z, k = col // (2 * N_Z), lax.rem(col // 2, N_Z), lax.rem(col, 2)
     mine = x * 2 + k
-    gath = (gath0, gath1)
+    gath = (gath0, gath1, gath2, gath3)
     live = count_ref[0]
+    side = z // 2
+    outer = lax.rem(z + 1, N_Z) < 2
+    partner = z + 1 - 2 * lax.rem(z, 2)
+    far_outer = 3 * (1 - side)
+    goals = (2 - side, far_outer, partner, z)
 
     def plane(o):
         return lax.rem(x + o // 2, N_X) * 2 + lax.rem(k + lax.rem(o, 2), 2)
@@ -79,8 +88,8 @@
     hi_row = (1 - z_hi) * N_Y + y
     hi_dev = {"row": hi_row, "col": col}
 
-    def z_dev(d):
-        return {"row": row, "col": x * (2 * N_Z) + lax.rem(z + d, N_Z) * 2 + k}
+    def z_dev(to):
+        return {"row": row, "col": x * (2 * N_Z) + to * 2 + k}
 
     loads = [
         pltpu.make_async_copy(src, dst, load_sem.at[i])
@@ -100,22 +109,30 @@
         load.start()
 
     barrier = pltpu.get_barrier_semaphore()
-    peers = [hi_dev, y_dev(1), y_dev(N_Y - 1)] + [z_dev(d) for d in range(1, N_Z)]
+    peers = [hi_dev, y_dev(1), y_dev(N_Y - 1)] + [z_dev(lax.rem(z + d, N_Z)) for d in range(1, N_Z)]
     peers += [plane_dev(plane(o)) for o in range(1, 8)]
     for peer in peers:
         pl.semaphore_signal(barrier, inc=1, device_id=peer, device_id_type=MESH)
     feat[PER_DEV] = jnp.zeros((BLOCK, 2 * HALF), jnp.bfloat16)
-    for h in range(2):
-        gath[h][8 * PER_DEV] = jnp.zeros((BLOCK, HALF), jnp.bfloat16)
+    for g in range(PARTS):
+        gath[g][8 * DUOS] = jnp.zeros((BLOCK, HALF), jnp.bfloat16)
+    low = lax.broadcasted_iota(jnp.int32, (BLOCK, HALF), 1) < HALF // 2
+
+    def swap(value):
+        return jnp.concatenate([value[:, HALF // 2 :], value[:, : HALF // 2]], axis=1)
+
     load_feat.wait()
+    for d in range(DUOS):
+        for h in range(2):
+            even = feat[2 * d, :, pl.ds(h * HALF, HALF)]
+            odd = feat[2 * d + 1, :, pl.ds(h * HALF, HALF)]
+            packs[2 * h, d] = jnp.where(low, even, swap(odd))
+            packs[2 * h + 1, d] = jnp.where(low, swap(even), odd)
     load_rows.wait()
     pl.semaphore_wait(barrier, len(peers))
 
-    def share(h, r):
-        return gath[h].at[pl.ds(r * PER_DEV, PER_DEV)]
-
-    def half(h):
-        return feat.at[pl.ds(0, PER_DEV), :, pl.ds(h * HALF, HALF)]
+    def share(g, r):
+        return gath[g].at[pl.ds(r * DUOS, DUOS)]
 
     def copy(src, dst, send, recv, peer):
         return pltpu.make_async_remote_copy(
@@ -123,10 +140,10 @@
         )
 
     def place(h, hi, at_y, first, blocks):
-        return gath[h].at[pl.ds((hi * N_Y + at_y) * PER_DEV + first, blocks)]
+        return gath[h].at[pl.ds((hi * N_Y + at_y) * DUOS + first, blocks)]
 
     def hi_copy(h, c):
-        src = feat.at[pl.ds(c * SOME, SOME), :, pl.ds(h * HALF, HALF)]
+        src = packs.at[h, pl.ds(c * SOME, SOME)]
         return copy(src, place(h, z_hi, y, c * SOME, SOME), hi_send.at[h, c], hi_recv.at[h, c], hi_dev)
 
     def hi_arrival(h, c):
@@ -134,12 +151,12 @@
         return copy(dst, dst, hi_send.at[h, c], hi_recv.at[h, c], hi_dev)
 
     def piece(t):
-        return (z_hi, 0, PER_DEV) if t == 0 else (1 - z_hi, (t - 1) * SOME, SOME)
+        return (z_hi, 0, DUOS) if t == 0 else (1 - z_hi, (t - 1) * SOME, SOME)
 
     def y_copy(h, t, up):
         hi, first, blocks = piece(t)
         dst = place(h, hi, y, first, blocks)
-        src = half(h) if t == 0 else dst
+        src = packs.at[h] if t == 0 else dst
         return copy(src, dst, y_send.at[h, t, 0, up], y_recv.at[h, t, 0, up], y_dev(1 if up else N_Y - 1))
 
     def y_arrival(h, t, up):
@@ -183,26 +200,21 @@
         p = plane(o)
         return copy(ids.at[p], ids.at[p], id_send.at[p], id_recv.at[p], plane_dev(p))
 
-    def levels(u):
-        j = min(u, N_Z - 1)
-        return (j, range(LEVELS)) if u < N_Z - 1 else (j, range(2 * (u - j), 2 * (u - j) + 2))
-
-    def x_copy(h, u, o):
+    def x_copy(g, j, o):
         p = plane(o)
-        j, lvs = levels(u)
-        at = pl.ds(lvs[0], len(lvs))
-        return copy(
-            xs.at[h, j, o - 1, at], xr.at[h, j, mine, at], x_send.at[h, u, p], x_recv.at[h, u, mine], plane_dev(p)
-        )
-
-    def x_arrival(h, u, o):
+        return copy(xs.at[g, j, o - 1], xr.at[g, j, mine], x_send.at[g, j, p], x_recv.at[g, j, mine], plane_dev(p))
+
+    def x_arrival(g, j, o):
         p = plane(o)
-        j, lvs = levels(u)
-        dst = xr.at[h, j, p, pl.ds(lvs[0], len(lvs))]
-        return copy(dst, dst, x_send.at[h, u, p], x_recv.at[h, u, p], plane_dev(p))
+        return copy(xr.at[g, j, p], xr.at[g, j, p], x_send.at[g, j, p], x_recv.at[g, j, p], plane_dev(p))
 
     def z_copy(h, j):
-        return copy(zs.at[h, j], zr.at[h, j], z_send.at[h, j], z_recv.at[h, j], z_dev(STEPS[j]))
+        peer = jnp.where(outer, partner, far_outer) if j == 1 else goals[j]
+        slot = (jnp.where(outer, 1, 2), 0, 3)[j]
+        return copy(zs.at[h, j], zr.at[h, slot], z_send.at[h, j], z_recv.at[h, slot], z_dev(peer))
+
+    def z_arrival(h, slot):
+        return copy(zr.at[h, slot], zr.at[h, slot], z_send.at[h, 0], z_recv.at[h, slot], z_dev(partner))
 
     def over(n, body):
         def step(o, carry):
@@ -215,7 +227,7 @@
     hi_copy(0, 1).start()
     send_on(0, 0)
     over(8, lambda o: id_copy(o).start())
-    keeps = [pltpu.make_async_copy(half(h), share(h, row), share_sem.at[h]) for h in range(2)]
+    keeps = [pltpu.make_async_copy(packs.at[g], share(g, row), share_sem.at[g]) for g in range(PARTS)]
     for keep in keeps:
         keep.start()
 
@@ -256,78 +268,95 @@
 
         lax.fori_loop(0, BLOCK // GROUP, some, 0)
 
-    load_near.wait()
-    near(0)
-    pass_on(0, 0)
-    hi_then_y(0, 0)
-    over(8, lambda o: id_arrival(o).wait_recv())
-    for j in range(N_Z):
-        to = lax.rem(z + STEPS[j], N_Z)
-        slot = lax.rem(lane, BLOCK // 2) // GROUP * 32 + x * (2 * N_Z) + to * 2 + k
-        for c in range(N_X):
+    def build(j):
+        to = goals[j]
+        level = 2 * (lax.rem(lane, 2 * GROUP) // GROUP)
+        for c in range(4):
+            slot = (level + c // 2) * 32 + x * (2 * N_Z) + to * 2 + k
             block = 0.0
-            for i in range(2):
-                wanted = (line == 2 * slot + 1) & (lane // (BLOCK // 2) == i)
-                block += spread(2 * c + i, wanted)
+            for i in range(4):
+                wanted = (line == 2 * slot + 1) & (lane // (2 * GROUP) == i)
+                block += spread(4 * (c % 2) + i, wanted)
             pick[j, :, pl.ds(c * BLOCK, BLOCK)] = picker(block)
 
-    load_far.wait()
-    for keep in keeps:
-        keep.wait()
-    hi_then_y(0, 1)
-    hi_copy(1, 0).start()
-    hi_copy(1, 1).start()
-    pass_on(0, 1)
-    pass_on(0, 2)
-    send_on(1, 0)
-    gathered(0)
-
-    def product(h, j, p, lv):
-        to = lax.rem(z + STEPS[j], N_Z)
-        slot = lv * 32 + (p // 2) * (2 * N_Z) + to * 2 + lax.rem(p, 2)
-        src = jnp.where(2 * slot + 1 < live, col_ref[2 * slot + 1], 8 * PER_DEV)
-        out = jnp.dot(far_tiles[slot], gath[h][src], preferred_element_type=jnp.float32)
+    def product(g, j, p, e):
+        to = goals[j]
+        left, right = [], []
+        for i in range(2):
+            slot = (2 * e + i) * 32 + (p // 2) * (2 * N_Z) + to * 2 + lax.rem(p, 2)
+            src = jnp.where(2 * slot + 1 < live, col_ref[2 * slot + 1], 8 * PER_DEV)
+            block = gath[g][lax.div(src, 2)]
+            block = jnp.where(lax.rem(src, 2) == i, block, swap(block))
+            left.append(far_tiles[slot])
+            right.append(jnp.where(low if i == 0 else ~low, block, jnp.zeros_like(block)))
+        out = jnp.dot(
+            jnp.concatenate(left, axis=1), jnp.concatenate(right, axis=0), preferred_element_type=jnp.float32
+        )
         return out.astype(jnp.bfloat16)
 
-    def multiply(h, u):
-        j, lvs = levels(u)
-
+    def multiply(g, j):
         def one(o):
-            for lv in lvs:
-                xs[h, j, o - 1, lv] = product(h, j, plane(o), lv)
-            x_copy(h, u, o).start()
+            for e in range(LEVELS // 2):
+                xs[g, j, o - 1, e] = product(g, j, plane(o), e)
+            x_copy(g, j, o).start()
 
         over(8, one)
-        for lv in lvs:
-            xr[h, j, mine, lv] = product(h, j, mine, lv)
+        for e in range(LEVELS // 2):
+            xr[g, j, mine, e] = product(g, j, mine, e)
 
     def combine(h, j):
-        for u in (j,) if j < N_Z - 1 else (j, j + 1):
-            over(8, lambda o: x_arrival(h, u, o).wait_recv())
+        for g in (2 * h, 2 * h + 1):
+            over(8, lambda o: x_arrival(g, j, o).wait_recv())
+        lows = lax.broadcasted_iota(jnp.int32, (8 * LEVELS // 2 * GROUP, HALF), 1) < HALF // 2
 
         def some(g, carry):
             rows = pl.ds(pl.multiple_of(g * GROUP, GROUP), GROUP)
-            arrived = xr[h, j, :, :, rows, :].reshape(8 * LEVELS * GROUP, HALF)
-            total = jnp.dot(pick[j], arrived, preferred_element_type=jnp.float32)
+            one, two = [xr[2 * h + i, j, :, :, rows, :].reshape(8 * LEVELS // 2 * GROUP, HALF) for i in range(2)]
+            arrived = [jnp.where(lows, one, swap(two)), jnp.where(lows, swap(one), two)]
+            total = jnp.dot(pick[j], jnp.concatenate(arrived, axis=0), preferred_element_type=jnp.float32)
             total = total.reshape(PER_DEV, GROUP, HALF)
             if j < N_Z - 1:
                 zs[h, j, :, rows, :] = total.astype(jnp.bfloat16)
-            else:
+            if j % 2:
                 own[h, :, rows, :] = total
             return carry
 
         lax.fori_loop(0, BLOCK // GROUP, some, 0)
-        if j < N_Z - 1:
+        if j == 1:
+            pl.when(outer)(z_copy(h, j).start)
+        elif j < N_Z - 1:
             z_copy(h, j).start()
 
+    def merge(h):
+        @pl.when(jnp.logical_not(outer))
+        def _():
+            z_arrival(h, 0).wait_recv()
+
+            def some(b, carry):
+                zs[h, 1, b] = (own[h, b] + zr[h, 0, b].astype(jnp.float32)).astype(jnp.bfloat16)
+                return carry
+
+            lax.fori_loop(0, PER_DEV, some, 0)
+            z_copy(h, 1).start()
+
     def finish(h):
-        for j in range(N_Z - 1):
-            z_copy(h, j).wait_recv()
+        z_arrival(h, 3).wait_recv()
+
+        @pl.when(outer)
+        def _():
+            z_arrival(h, 0).wait_recv()
+
+        @pl.when(jnp.logical_not(outer))
+        def _():
+            z_arrival(h, 1).wait_recv()
+            z_arrival(h, 2).wait_recv()
+
+        slots = (3, jnp.where(outer, 0, 1), jnp.where(outer, 4, 2))
 
         def some(b, carry):
             total = own[h, b] + near_sum[b, :, pl.ds(h * HALF, HALF)]
-            for j in range(N_Z - 1):
-                total += zr[h, j, b].astype(jnp.float32)
+            for slot in slots:
+                total += zr[h, slot, b].astype(jnp.float32)
             part = jnp.dot(
                 total.astype(jnp.bfloat16),
                 weight[pl.ds(h * HALF, HALF), :],
@@ -342,46 +371,100 @@
 
         lax.fori_loop(0, PER_DEV, some, 0)
 
+    def onward(g):
+        pass_on(g, 0)
+        hi_then_y(g, 0)
+        hi_then_y(g, 1)
+        start_hi(g + 1)
+        pass_on(g, 1)
+        pass_on(g, 2)
+        if g + 1 < PARTS:
+            send_on(g + 1, 0)
+
+    def start_hi(g):
+        if 0 < g < PARTS:
+            for c in range(2):
+                hi_copy(g, c).start()
+
+    onward(0)
+    over(8, lambda o: id_arrival(o).wait_recv())
+    build(0)
+    load_far.wait()
+    for keep in keeps:
+        keep.wait()
+    gathered(0)
     multiply(0, 0)
     multiply(0, 1)
+    pass_on(1, 0)
     hi_then_y(1, 0)
     multiply(0, 2)
-    pass_on(1, 0)
     hi_then_y(1, 1)
-    multiply(0, 3)
-    combine(0, 0)
+    start_hi(2)
+    build(1)
     pass_on(1, 1)
     pass_on(1, 2)
-    combine(0, 1)
+    send_on(2, 0)
+    build(2)
     gathered(1)
     multiply(1, 0)
+    multiply(1, 1)
+    pass_on(2, 0)
+    hi_then_y(2, 0)
+    multiply(1, 2)
+    hi_then_y(2, 1)
+    start_hi(3)
+    combine(0, 0)
+    pass_on(2, 1)
+    pass_on(2, 2)
+    send_on(3, 0)
+    multiply(0, 3)
+    combine(0, 1)
+    build(3)
     combine(0, 2)
-    multiply(1, 1)
-    multiply(1, 2)
-    multiply(0, 4)
+    gathered(2)
+    multiply(2, 0)
+    pass_on(3, 0)
+    hi_then_y(3, 0)
+    multiply(2, 1)
+    hi_then_y(3, 1)
+    multiply(2, 2)
+    merge(0)
+    pass_on(3, 1)
+    pass_on(3, 2)
+    for h in range(2):
+        zr[h, 4] = jnp.zeros((PER_DEV, BLOCK, HALF), jnp.bfloat16)
+    gathered(3)
+    multiply(3, 0)
+    multiply(3, 1)
+    multiply(3, 2)
+    combine(1, 0)
     multiply(1, 3)
-    multiply(1, 4)
-    combine(1, 0)
-    near(1)
     combine(1, 1)
+    multiply(2, 3)
+    multiply(3, 3)
+    combine(1, 2)
+    load_near.wait()
+    near(0)
     load_weight.wait()
     load_bias.wait()
-    combine(1, 2)
+    merge(1)
+    near(1)
     combine(0, 3)
     finish(0)
     combine(1, 3)
     finish(1)
 
     over(8, lambda o: id_copy(o).wait_send())
-    for h in range(2):
+    for g in range(PARTS):
         for c in range(2):
-            hi_copy(h, c).wait_send()
+            hi_copy(g, c).wait_send()
         for t in range(3):
             for up in (0, 1):
-                y_copy(h, t, up).wait_send()
-                on_copy(h, t, up).wait_send()
-        for u in range(N_Z + 1):
-            over(8, lambda o: x_copy(h, u, o).wait_send())
+                y_copy(g, t, up).wait_send()
+                on_copy(g, t, up).wait_send()
+        for j in range(N_Z):
+            over(8, lambda o: x_copy(g, j, o).wait_send())
+    for h in range(2):
         for j in range(N_Z - 1):
             z_copy(h, j).wait_send()
 
@@ -397,9 +480,9 @@
         in_specs=[smem, smem, hbm, hbm, hbm, hbm, hbm],
         out_specs=vmem,
         scratch_shapes=[
-            pltpu.VMEM((8 * PER_DEV + 1, BLOCK, HALF), jnp.bfloat16),
-            pltpu.VMEM((8 * PER_DEV + 1, BLOCK, HALF), jnp.bfloat16),
+            *[pltpu.VMEM((8 * DUOS + 1, BLOCK, HALF), jnp.bfloat16)] * PARTS,
             pltpu.VMEM((PER_DEV + 1, BLOCK, 2 * HALF), jnp.bfloat16),
+            pltpu.VMEM((PARTS, DUOS, BLOCK, HALF), jnp.bfloat16),
             pltpu.VMEM((PAIRS, BLOCK, BLOCK), jnp.bfloat16),
             pltpu.VMEM((PAIRS, BLOCK, BLOCK), jnp.bfloat16),
             pltpu.VMEM((2 * HALF, 2 * HALF), jnp.bfloat16),
@@ -409,24 +492,24 @@
             pltpu.VMEM((PER_DEV * GROUP, PART * GROUP), jnp.bfloat16),
             pltpu.VMEM((PART, BLOCK, 2 * HALF), jnp.bfloat16),
             pltpu.VMEM((PER_DEV, BLOCK, 2 * HALF), jnp.float32),
-            pltpu.VMEM((2, N_Z, 7, LEVELS, BLOCK, HALF), jnp.bfloat16),
-            pltpu.VMEM((2, N_Z, 8, LEVELS, BLOCK, HALF), jnp.bfloat16),
+            pltpu.VMEM((PARTS, N_Z, 7, LEVELS // 2, BLOCK, HALF), jnp.bfloat16),
+            pltpu.VMEM((PARTS, N_Z, 8, LEVELS // 2, BLOCK, HALF), jnp.bfloat16),
             pltpu.VMEM((2, N_Z - 1, PER_DEV, BLOCK, HALF), jnp.bfloat16),
-            pltpu.VMEM((2, N_Z - 1, PER_DEV, BLOCK, HALF), jnp.bfloat16),
+            pltpu.VMEM((2, N_Z + 1, PER_DEV, BLOCK, HALF), jnp.bfloat16),
             pltpu.VMEM((2, PER_DEV, BLOCK, HALF), jnp.float32),
             pltpu.VMEM((ROWS, 2 * HALF), jnp.float32),
             dma((6,)),
-            dma((2,)),
-            dma((2, 2)),
-            dma((2, 2)),
-            dma((2, 3, 2, 2)),
-            dma((2, 3, 2, 2)),
+            dma((PARTS,)),
+            dma((PARTS, 2)),
+            dma((PARTS, 2)),
+            dma((PARTS, 3, 2, 2)),
+            dma((PARTS, 3, 2, 2)),
             dma((8,)),
             dma((8,)),
-            dma((2, N_Z + 1, 8)),
-            dma((2, N_Z + 1, 8)),
+            dma((PARTS, N_Z, 8)),
+            dma((PARTS, N_Z, 8)),
             dma((2, N_Z - 1)),
-            dma((2, N_Z - 1)),
+            dma((2, N_Z)),
         ],
         compiler_params=pltpu.CompilerParams(
             collective_id=0, has_side_effects=True, vmem_limit_bytes=60 * 2**20

time: 167 us -> 159 us (0.952); the launches traced: 164 us -> 159 us
  Pallas kernels: 160 us -> 155 us
    pallas_call x1, Pallas kernels: 160 us -> 155 us  [far(): pl.pallas_call(far_kernel, out_shape=jax.ShapeDtypeStruct((ROWS, 2 * HALF...]
where the time goes in v4:
time: 159 us
  Pallas kernels  155 us (97%)
  local copies, waits for them, and re-layouts  2.86 us (2%)
    pallas_call x1, Pallas kernels, far(): pl.pallas_call(far_kernel, out_shape=jax.ShapeDtypeStruct((ROWS, 2 * HALF...  155 us

profile of v4, /device:TPU:1, one launch (start us, length us, event | category | flops | bytes accessed | tf_op | source)
XLA Modules:
  0.0 159.2 jit_solution(11664512423040693223)
XLA Ops:
  0.7 0.7 fusion.1
  1.3 0.6 broadcast_in_dim.3.rows_ref
  1.9 155.0 %shard_map.73 = bf16[2048,256]{1,0:T(8,128)(2,1)} custom-call(s32[1]{0:T(128)S(6)} %copy.9.count_ref, s32[256]{0:T(256)} %col_ref.1, bf16[16,128,256]{2,1,0:T(8,128)(2,1)} %bitcast.4, f32[8,256]{1,0:T(8,128)} %broadcast_in_dim.3.rows_ref, bf16[256,256]{1,0:T(8,128)(2,1)} %weight_ref.1, f32[1,256]{1,0:T(1,128)} %bitcast.5, bf16[128,2,128,128]{3,2,1,0:T(8,128)(2,1)} %bitcast.3), custom_call_target="tpu_custom_call" | custom-call | tf_op jit(solution)/shard_map/pallas_call | solution.py:477
  156.9 2.3 %copy.10 = bf16[2048,256]{1,0:T(8,128)(2,1)} copy(bf16[2048,256]{1,0:T(8,128)(2,1)} %shard_map.73) | data formatting | bytes 2097152

commit v5 on v4

--- a/solution.py
+++ b/solution.py
@@ -407,12 +407,12 @@
     build(2)
     gathered(1)
     multiply(1, 0)
-    multiply(1, 1)
     pass_on(2, 0)
     hi_then_y(2, 0)
-    multiply(1, 2)
+    multiply(1, 1)
     hi_then_y(2, 1)
     start_hi(3)
+    multiply(1, 2)
     combine(0, 0)
     pass_on(2, 1)
     pass_on(2, 2)
@@ -420,19 +420,19 @@
     multiply(0, 3)
     combine(0, 1)
     build(3)
-    combine(0, 2)
     gathered(2)
     multiply(2, 0)
     pass_on(3, 0)
     hi_then_y(3, 0)
+    hi_then_y(3, 1)
     multiply(2, 1)
-    hi_then_y(3, 1)
+    combine(0, 2)
     multiply(2, 2)
-    merge(0)
     pass_on(3, 1)
     pass_on(3, 2)
-    for h in range(2):
-        zr[h, 4] = jnp.zeros((PER_DEV, BLOCK, HALF), jnp.bfloat16)
+    zr[0, 4] = jnp.zeros((PER_DEV, BLOCK, HALF), jnp.bfloat16)
+    zr[1, 4] = jnp.zeros((PER_DEV, BLOCK, HALF), jnp.bfloat16)
+    merge(0)
     gathered(3)
     multiply(3, 0)
     multiply(3, 1)

time: 159 us -> 155 us (0.975)
  Pallas kernels: 155 us -> 151 us
    pallas_call x1, Pallas kernels: 155 us -> 151 us  [far(): pl.pallas_call(far_kernel, out_shape=jax.ShapeDtypeStruct((ROWS, 2 * HALF...]
where the time goes in v5:
time: 155 us
  Pallas kernels  151 us (97%)
  local copies, waits for them, and re-layouts  2.86 us (2%)
    pallas_call x1, Pallas kernels, far(): pl.pallas_call(far_kernel, out_shape=jax.ShapeDtypeStruct((ROWS, 2 * HALF...  151 us

profile of v5, /device:TPU:1, one launch (start us, length us, event | category | flops | bytes accessed | tf_op | source)
XLA Modules:
  0.0 155.3 jit_solution(9211950115271428046)
XLA Ops:
  0.7 0.7 fusion.1
  1.3 0.6 broadcast_in_dim.3.rows_ref
  1.9 151.1 %shard_map.73 = bf16[2048,256]{1,0:T(8,128)(2,1)} custom-call(s32[1]{0:T(128)S(6)} %copy.9.count_ref, s32[256]{0:T(256)} %col_ref.1, bf16[16,128,256]{2,1,0:T(8,128)(2,1)} %bitcast.4, f32[8,256]{1,0:T(8,128)} %broadcast_in_dim.3.rows_ref, bf16[256,256]{1,0:T(8,128)(2,1)} %weight_ref.1, f32[1,256]{1,0:T(1,128)} %bitcast.5, bf16[128,2,128,128]{3,2,1,0:T(8,128)(2,1)} %bitcast.3), custom_call_target="tpu_custom_call" | custom-call | tf_op jit(solution)/shard_map/pallas_call | solution.py:477
  153.0 2.3 %copy.10 = bf16[2048,256]{1,0:T(8,128)(2,1)} copy(bf16[2048,256]{1,0:T(8,128)(2,1)} %shard_map.73) | data formatting | bytes 2097152
